TPU v7x, 128 devices: a whole 4x4x4 slice. The times are simulated.
128 devices in a mesh: seq: 16 (over x_lo, z, core), fsdp: 8 (over y, x_hi).
Axes of the slice: x: 4 (x_hi: 2, x_lo: 2; x = x_hi * 2 + x_lo), y: 4, z: 4, core: 2. Of those that a mesh axis runs over, the one named last changes fastest.
Arguments:
- perturbed_codes: float32 [16, 1024, 2432], P('fsdp', 'seq'), may hold values from -6 to 6
- random_draws: float32 [2, 16, 1024, 2432], P(None, 'fsdp', 'seq'), may hold values from -6 to 6
- relative_rewards: float32 [16], P('fsdp'), may hold values from -4 to 4
- rescaling_gains: bfloat16 [2432], replicated, may hold values from 0.5 to 1.5
- triple_projector: bfloat16 [2432, 6144], P(None, 'seq'), may hold values from -2 to 2
- emission_projector: bfloat16 [2048, 2432], replicated, may hold values from -0.125 to 0.125
- payload_bypass_reducer: bfloat16 [2432, 32], replicated, may hold values from -0.125 to 0.125
- payload_bypass_lift: bfloat16 [32, 2048], replicated, may hold values from -1 to 1
- outlet_bypass_reducer: bfloat16 [2048, 32], replicated, may hold values from -0.125 to 0.125
- outlet_bypass_lift: bfloat16 [32, 2432], replicated, may hold values from -1 to 1
Outputs:
- ending_diffusion_image: float32 [16, 1024, 2432], P('fsdp', 'seq')
- grad_av: float32 [2432, 32], P(('seq', 'fsdp'))
- grad_bv: float32 [32, 2048], P(None, ('seq', 'fsdp'))
- outlet_reducer_derivative: float32 [2048, 32], P(('seq', 'fsdp'))
- output_up_gradient: float32 [32, 2432], P(None, ('seq', 'fsdp'))
All inputs are finite; a program needn't handle non-finite values.
Results may differ from a plain program's by a relative error of at most 0.017.
Values may be sent and summed in bfloat16 or wider, within the bound.
A program may use at most 192 MiB of HBM per device.

v0:
```python
import math

import jax
import jax.numpy as jnp
from jax import lax
from jax.sharding import PartitionSpec as P

FOCUS_BRANCHES = 32
BRANCH_SPAN = 64


TIMES = (0.8, 0.7)
STEP = -0.1
LEVEL = 0.7
EPS = 1e-06


def plan(index):
    moment = TIMES[index]
    sigma = LEVEL * math.sqrt(moment / (1.0 - moment))
    drift = sigma * sigma / (2.0 * moment)
    spread = sigma * math.sqrt(-STEP)
    keep = 1.0 + STEP * drift
    push = STEP * (1.0 + drift * (1.0 - moment))
    return (keep, push, spread)


def normed(current_iterate, rescaling_gains):
    power = jnp.mean(current_iterate * current_iterate, axis=-1, keepdims=True)
    return (current_iterate * lax.rsqrt(power + EPS) * rescaling_gains.astype(jnp.float32)).astype(
        jnp.bfloat16
    )


def attend(mixed):
    items, length, columns = mixed.shape
    heads_here = columns // (3 * BRANCH_SPAN)
    mixed = mixed.reshape(items, length, heads_here, 3, BRANCH_SPAN)
    scores = jnp.einsum(
        "bqhe,bkhe->bhqk",
        mixed[:, :, :, 0, :],
        mixed[:, :, :, 1, :],
        preferred_element_type=jnp.float32,
    ) * BRANCH_SPAN ** (-0.5)
    probs = jax.nn.softmax(scores, axis=-1).astype(jnp.bfloat16)
    blended_lookup_answer = jnp.einsum(
        "bhqk,bkhe->bqhe", probs, mixed[:, :, :, 2, :], preferred_element_type=jnp.float32
    )
    return (
        blended_lookup_answer.astype(jnp.bfloat16).reshape(items, length, heads_here * BRANCH_SPAN),
        probs,
    )


def per_device(
    perturbed_codes,
    random_draws,
    relative_rewards,
    rescaling_gains,
    triple_projector,
    emission_projector,
    payload_bypass_reducer,
    payload_bypass_lift,
    outlet_bypass_reducer,
    outlet_bypass_lift,
):
    items, local, width = perturbed_codes.shape
    groups = lax.axis_size("seq")
    samples = items * lax.axis_size("fsdp")
    heads_here = FOCUS_BRANCHES // groups
    partition_channel_band = heads_here * BRANCH_SPAN
    length = local * groups
    full_weight = lax.all_gather(triple_projector, "seq", axis=1, tiled=True)
    current_iterate = perturbed_codes
    saved = []
    for index in range(2):
        keep, push, spread = plan(index)
        hidden_rows = normed(current_iterate, rescaling_gains)
        payload_thin_lines = jnp.einsum(
            "ohp,pl->ohl", hidden_rows, payload_bypass_reducer, preferred_element_type=jnp.float32
        ).astype(jnp.bfloat16)
        mixed = jnp.einsum(
            "bsd,dc->bsc", hidden_rows, full_weight, preferred_element_type=jnp.float32
        ).reshape(items, local, FOCUS_BRANCHES, 3, BRANCH_SPAN)
        iterate_increment = jnp.einsum(
            "bys,sx->byx",
            payload_thin_lines,
            payload_bypass_lift,
            preferred_element_type=jnp.float32,
        ).reshape(items, local, FOCUS_BRANCHES, BRANCH_SPAN)
        mixed = (
            mixed.at[:, :, :, 2, :]
            .add(iterate_increment)
            .astype(jnp.bfloat16)
            .reshape(items, local, 3 * FOCUS_BRANCHES * BRANCH_SPAN)
        )
        attended_heads, probs = attend(
            lax.all_to_all(mixed, "seq", split_axis=2, concat_axis=1, tiled=True)
        )
        blended_lookup_answer = lax.all_to_all(
            attended_heads, "seq", split_axis=1, concat_axis=2, tiled=True
        )
        outlet_thin_operand = jnp.einsum(
            "hnd,do->hno",
            blended_lookup_answer,
            outlet_bypass_reducer,
            preferred_element_type=jnp.float32,
        ).astype(jnp.bfloat16)
        predicted_velocity = jnp.einsum(
            "bsc,cd->bsd",
            blended_lookup_answer,
            emission_projector,
            preferred_element_type=jnp.float32,
        ) + jnp.einsum(
            "ief,fm->iem",
            outlet_thin_operand,
            outlet_bypass_lift,
            preferred_element_type=jnp.float32,
        )
        saved.append(
            (hidden_rows, payload_thin_lines, blended_lookup_answer, outlet_thin_operand, probs)
        )
        current_iterate = (
            keep * current_iterate + push * predicted_velocity + spread * random_draws[index]
        )
    outlet_reducer_derivative = jnp.zeros(outlet_bypass_reducer.shape, jnp.float32)
    output_up_gradient = jnp.zeros(outlet_bypass_lift.shape, jnp.float32)
    douts = []
    for index in range(2):
        keep, push, spread = plan(index)
        hidden_rows, payload_thin_lines, blended_lookup_answer, outlet_thin_operand, probs = saved[
            index
        ]
        coef = -push / (2.0 * samples * spread)
        drift_field_derivative = (
            (coef * relative_rewards)[:, None, None] * random_draws[index]
        ).astype(jnp.bfloat16)
        output_up_gradient = output_up_gradient + jnp.einsum(
            "bsr,bsc->rc",
            outlet_thin_operand,
            drift_field_derivative,
            preferred_element_type=jnp.float32,
        )
        emitted_thin_derivative = jnp.einsum(
            "pwm,nm->pwn",
            drift_field_derivative,
            outlet_bypass_lift,
            preferred_element_type=jnp.float32,
        ).astype(jnp.bfloat16)
        outlet_reducer_derivative = outlet_reducer_derivative + jnp.einsum(
            "bsc,bsr->cr",
            blended_lookup_answer,
            emitted_thin_derivative,
            preferred_element_type=jnp.float32,
        )
        emitted_derivative = jnp.einsum(
            "bsc,ec->bse",
            drift_field_derivative,
            emission_projector,
            preferred_element_type=jnp.float32,
        ) + jnp.einsum(
            "tod,ld->tol",
            emitted_thin_derivative,
            outlet_bypass_reducer,
            preferred_element_type=jnp.float32,
        )
        douts.append(emitted_derivative.astype(jnp.bfloat16))
    dout_all = jnp.stack(douts)
    probs_all = jnp.stack([saved[0][4], saved[1][4]])
    dheads = lax.all_to_all(dout_all, "seq", split_axis=3, concat_axis=2, tiled=True)
    dheads = dheads.reshape(2, items, length, heads_here, BRANCH_SPAN)
    payload_derivative_lines = jnp.einsum(
        "nbhqk,nbqhe->nbkhe", probs_all, dheads, preferred_element_type=jnp.float32
    )
    payload_derivative_lines = payload_derivative_lines.astype(jnp.bfloat16).reshape(
        2, items, length, partition_channel_band
    )
    hiddens = jnp.stack([saved[0][0], saved[1][0]])
    low_vs = jnp.stack([saved[0][1], saved[1][1]])
    payload_derivative_lines = lax.all_to_all(
        payload_derivative_lines, "seq", split_axis=2, concat_axis=3, tiled=True
    )
    grad_bv = jnp.einsum(
        "nbsr,nbsc->rc", low_vs, payload_derivative_lines, preferred_element_type=jnp.float32
    )
    payload_thin_derivative = jnp.einsum(
        "gwpy,vy->gwpv",
        payload_derivative_lines,
        payload_bypass_lift,
        preferred_element_type=jnp.float32,
    ).astype(jnp.bfloat16)
    grad_av = jnp.einsum(
        "nbsd,nbsr->dr", hiddens, payload_thin_derivative, preferred_element_type=jnp.float32
    )
    grad_av, grad_bv, outlet_reducer_derivative, output_up_gradient = (
        lax.psum_scatter(grad_av, ("seq", "fsdp"), scatter_dimension=0, tiled=True),
        lax.psum_scatter(grad_bv, ("seq", "fsdp"), scatter_dimension=1, tiled=True),
        lax.psum_scatter(
            outlet_reducer_derivative, ("seq", "fsdp"), scatter_dimension=0, tiled=True
        ),
        lax.psum_scatter(output_up_gradient, ("seq", "fsdp"), scatter_dimension=1, tiled=True),
    )
    return (current_iterate, grad_av, grad_bv, outlet_reducer_derivative, output_up_gradient)


def solution(mesh):
    placed = (
        P("fsdp", "seq", None),
        P(None, "fsdp", "seq", None),
        P("fsdp"),
        P(),
        P(None, "seq"),
        P(),
        P(),
        P(),
        P(),
        P(),
    )
    return jax.shard_map(
        per_device,
        mesh=mesh,
        in_specs=placed,
        out_specs=(
            P("fsdp", "seq", None),
            P(("seq", "fsdp"), None),
            P(None, ("seq", "fsdp")),
            P(("seq", "fsdp"), None),
            P(None, ("seq", "fsdp")),
        ),
        check_vma=False,
    )
```

profile of v0, /device:TPU:1, one launch (start us, length us, event | category | flops | bytes accessed | tf_op | source)
XLA Modules:
  0.0 2028.5 jit_solution(2405174275973588812)
XLA Ops:
  13.6 8.3 fusion.16
  21.9 144.6 %all-gather.2.cloned.1.call-done = bf16[2432,6144]{1,0:T(8,128)(2,1)} async-done(((bf16[2432,384]{1,0:T(8,128)(2,1)}), bf16[2432,6144]{1,0:T(8,128)(2,1)}) %all-gather.2.cloned.1.call-update) | async-done | bytes 29884432 | tf_op jit(solution)/shard_map/all_gather | solution.py:73
  166.5 15.5 fusion.4
  182.0 9.5 reshape.149
  191.5 8.7 slice_add_fusion.1
  200.2 53.0 %scatter-add.6 = f32[2,64,32,3,64]{4,3,2,1,0:T(4,128)} dynamic-update-slice(f32[2,64,32,3,64]{4,3,2,1,0:T(4,128)} %reshape.149, f32[2,64,32,1,64]{4,3,2,1,0:T(1,128)} %slice_add_fusion.1, s32[]{:T(128)} %constant.66.clone.1, s32[]{:T(128)} %constant.66.clone.1, s32[]{:T(128)} %constant.66.clone.1, s32[]{:T(128)} %constant.67.clone.1, s32[]{:T(128)} %constant.66.clone.1) | dynamic-update-slice | bytes 2097156 | tf_op jit(solution)/shard_map/scatter-add | solution.py:93
  253.1 7.4 convert_element_type.76
  260.5 11.7 copy.81
  284.9 7.1 fusion.18
  296.2 5.8 reshape.178
  325.7 9.8 fusion.82
  335.5 8.3 convolution_convert_fusion.1
  345.8 6.0 all-to-all-start.1
  364.7 5.7 fusion.22
  371.9 15.5 fusion.2
  387.4 9.6 reshape.154
  399.6 8.7 slice_add_fusion
  408.3 53.0 %scatter-add.9 = f32[2,64,32,3,64]{4,3,2,1,0:T(4,128)} dynamic-update-slice(f32[2,64,32,3,64]{4,3,2,1,0:T(4,128)} %reshape.154, f32[2,64,32,1,64]{4,3,2,1,0:T(1,128)} %slice_add_fusion, s32[]{:T(128)} %constant.66.clone.1, s32[]{:T(128)} %constant.66.clone.1, s32[]{:T(128)} %constant.66.clone.1, s32[]{:T(128)} %constant.67.clone.1, s32[]{:T(128)} %constant.66.clone.1) | dynamic-update-slice | bytes 2097156 | tf_op jit(solution)/shard_map/scatter-add | solution.py:93
  461.2 7.4 convert_element_type.83
  468.7 11.7 copy.82
  485.3 6.3 all-to-all-start.2
  491.6 9.7 fusion.109
  501.3 12.0 all-to-all-done.2
  529.3 9.8 fusion.83
  539.0 7.7 convolution_convert_fusion
  560.7 9.9 fusion.42
  575.1 5.7 all-to-all-start.5
  584.9 11.9 all-to-all-done.5
  608.7 6.5 fusion.20
  620.1 137.2 %all-reduce.5.cloned.1.call-done = (f32[2432,32]{1,0:T(8,128)}, f32[32,2432]{0,1:T(8,128)}) async-done(((f32[2432,32]{1,0:T(8,128)}, f32[32,2432]{0,1:T(8,128)}), (f32[2432,32]{1,0:T(8,128)}, f32[32,2432]{0,1:T(8,128)})) %all-reduce.5.cloned.1.call-update) | async-done | bytes 622608
  759.9 626.9 %reduce-scatter.5.cloned.1.call-done = f32[16,32]{1,0:T(8,128)} async-done(((f32[2048,32]{1,0:T(8,128)}), f32[16,32]{1,0:T(8,128)}) %reduce-scatter.5.cloned.1.call-update) | async-done | bytes 2064 | tf_op jit(solution)/shard_map/reduce_scatter | solution.py:198
  1386.9 634.9 %reduce-scatter.3.cloned.1.call-done = f32[32,16]{0,1:T(8,128)} async-done(((f32[32,2048]{0,1:T(8,128)}), f32[32,16]{0,1:T(8,128)}) %reduce-scatter.3.cloned.1.call-update) | async-done | bytes 2064 | tf_op jit(solution)/shard_map/reduce_scatter | solution.py:197
  (133 shorter events, 128.3 us)
Async XLA Ops:
  7.2 275.3 %copy-start = (bf16[32,2432]{1,0:T(8,128)(2,1)S(1)}, bf16[32,2432]{1,0:T(8,128)(2,1)}, u32[]{:S(2)}) copy-start(bf16[32,2432]{1,0:T(8,128)(2,1)} %param.23) | copy-start | bytes 466948
  7.2 1.5 copy-start.14
  7.2 159.3 %all-gather.2.cloned.1.call-start = ((), (), s32[]{:S(2)}) async-start(), calls=%async_computation.8 | async-start | bytes 31752192 | tf_op jit(solution)/shard_map/all_gather | solution.py:73
  9.2 2.5 copy-start.19
  9.5 2.2 copy-start.32
  13.6 268.8 %copy-start.3 = (bf16[2,64,2432]{2,1,0:T(8,128)(2,1)}, bf16[2,64,2432]{2,1,0:T(8,128)(2,1)S(1)}, u32[]{:S(2)}) copy-start(bf16[2,64,2432]{2,1,0:T(8,128)(2,1)S(1)} %get-tuple-element.32) | copy-start | bytes 1867780
  277.2 5.7 copy-start.17
  277.2 27.2 %all-to-all-start = ((bf16[16,2,24576]{2,1,0:T(2,128)(2,1)}), bf16[16,2,24576]{2,1,0:T(2,128)(2,1)}, u32[]{:S(2)}, u32[]{:S(2)}) async-start(bf16[16,2,24576]{2,1,0:T(2,128)(2,1)} %reshape.174), calls=%async_computation | async-start | bytes 3145728 | tf_op jit(solution)/shard_map/all_to_all | solution.py:98
  282.9 9.1 copy-start.23
  284.8 7.2 copy-start.25
  304.4 41.5 %all-to-all-start.4 = ((bf16[16,2,16384]{2,1,0:T(2,128)(2,1)}), bf16[16,2,16384]{2,1,0:T(2,128)(2,1)S(1)}, u32[]{:S(2)}, u32[]{:S(2)}) async-start(bf16[16,2,16384]{2,1,0:T(2,128)(2,1)} %reshape.178), calls=%async_computation.4 | async-start | bytes 2097152 | tf_op jit(solution)/shard_map/all_to_all | solution.py:170
  345.8 17.7 all-to-all-start.1
  364.7 5.7 copy-start.6
  364.7 6.0 copy-start.5
  371.9 25.1 %copy-start.21 = (bf16[2,64,32]{1,2,0:T(8,128)(2,1)}, bf16[2,64,32]{1,2,0:T(8,128)(2,1)S(1)}, u32[]{:S(2)}) copy-start(bf16[2,64,32]{1,2,0:T(8,128)(2,1)S(1)} %convolution_convert_fusion.6) | copy-start | bytes 24580
  387.4 9.6 copy-start.16
  485.3 28.0 %all-to-all-start.2 = ((bf16[16,2,24576]{2,1,0:T(2,128)(2,1)}), bf16[16,2,24576]{2,1,0:T(2,128)(2,1)}, u32[]{:S(2)}, u32[]{:S(2)}) async-start(bf16[16,2,24576]{2,1,0:T(2,128)(2,1)} %reshape.176), calls=%async_computation.2 | async-start | bytes 3145728 | tf_op jit(solution)/shard_map/all_to_all | solution.py:98
  539.0 10.7 copy-start.2
  555.8 18.5 all-to-all-start.3
  575.1 21.7 %all-to-all-start.5 = ((bf16[2,2,1024,128]{3,1,0,2:T(2,128)(2,1)}), bf16[2,2,1024,128]{3,1,0,2:T(2,128)(2,1)}, u32[]{:S(2)}, u32[]{:S(2)}) async-start(bf16[2,2,1024,128]{3,1,0,2:T(2,128)(2,1)} %copy.71), calls=%async_computation.5 | async-start | bytes 2097152 | tf_op jit(solution)/shard_map/all_to_all | solution.py:180
  580.8 1.8 copy-start.4
  580.8 176.5 %all-reduce.5.cloned.1.call-start = ((), (), s32[]{:S(2)}) async-start(), calls=%async_computation.11 | async-start | bytes 4980736
  582.6 2.3 copy-start.29
  599.7 2.4 copy-start.12
  599.7 2.4 copy-start.13
  605.9 781.0 %reduce-scatter.5.cloned.1.call-start = ((), (), s32[]{:S(2)}) async-start(), calls=%async_computation.10 | async-start | bytes 1056768 | tf_op jit(solution)/shard_map/reduce_scatter | solution.py:198
  608.6 6.6 copy-start.20
  608.6 6.6 copy-start.22
  608.6 1413.2 %reduce-scatter.3.cloned.1.call-start = ((), (), s32[]{:S(2)}) async-start(), calls=%async_computation.9 | async-start | bytes 1056768 | tf_op jit(solution)/shard_map/reduce_scatter | solution.py:197
  608.6 6.6 copy-start.9
  615.2 2.0 copy-start.8
  615.2 2.0 copy-start.30
  (11 other events, 11.5 us)
Sparse Core Ops, SparseCore 0:
  9.7 156.7 all-gather.1
  606.0 151.2 all-reduce.4
  760.3 626.4 reduce-scatter.4
  1389.6 632.1 reduce-scatter.2
where the time goes:
time: 2050 us; the launch traced here: 2030 us
  waiting for transfers between devices  1570 us (77%)
  local copies, waits for them, and re-layouts  236 us (12%)
  matrix products  122 us (6%)
  other arithmetic  51 us (2%)
  starting transfers between devices  34 us (2%)
    reduce_scatter x1, waiting for transfers between devices, per_device(): lax.psum_scatter(grad_bv, ('seq', 'fsdp'), scatter_dimension=1, tiled=True)  635 us
    reduce_scatter x1, waiting for transfers between devices, per_device(): lax.psum_scatter(outlet_reducer_derivative, ('seq', 'fsdp'), scatter_dime...  627 us
    all_gather x1, waiting for transfers between devices, per_device(): full_weight = lax.all_gather(triple_projector, 'seq', axis=1, tiled=True)  145 us
    unnamed x5, waiting for transfers between devices  138 us
    scatter-add x2, local copies, waits for them, and re-layouts, per_device(): mixed = mixed.at[:, :, :, 2, :].add(iterate_increment).astype(jnp.bfloat1...  106 us
  transfers between devices with their start and end apart: 10, of which 7 were waited for; matrix products, arithmetic and copies ran while one was open for 6% of the time, Pallas kernels for 0%

commit v1 on v0

v1 whole, which is shorter than its diff:
```python
import functools
import math

import jax
import jax.numpy as jnp
from jax import lax
from jax.experimental import pallas as pl
from jax.experimental.pallas import tpu as pltpu
from jax.sharding import PartitionSpec as P

TIMES = (0.8, 0.7)
STEP = -0.1
LEVEL = 0.7
EPS = 1e-06
SAMPLES = 16
WIDTH = 2432
INNER = 2048
RANK = 32
F32 = jnp.float32
BF16 = jnp.bfloat16
MESH = pl.DeviceIdType.MESH
NT = (((1,), (1,)), ((), ()))


def plan(index):
    moment = TIMES[index]
    sigma = LEVEL * math.sqrt(moment / (1.0 - moment))
    drift = sigma * sigma / (2.0 * moment)
    spread = sigma * math.sqrt(-STEP)
    keep = 1.0 + STEP * drift
    push = STEP * (1.0 + drift * (1.0 - moment))
    return (keep, push, spread)


def mm(a, b):
    return jnp.dot(a, b, preferred_element_type=F32)


def mm_nt(a, b):
    return lax.dot_general(a, b, NT, preferred_element_type=F32)


def remote(src, dst, send, recv, device):
    return pltpu.make_async_remote_copy(
        src_ref=src,
        dst_ref=dst,
        send_sem=send,
        recv_sem=recv,
        device_id=device,
        device_id_type=MESH,
    )


def block_kernel(
    x0, draws, rewards, gains, w_in, e_hbm, vred, vlift, ored, olift,
    x_out, r1_out, r2_out,
    wall, ep, hid, q, kv, lowvt, dout, dsend, dlo, dlo_src, redp, lift2,
    att, att_src, dvel, vt, dv, dlv, dl_src, dl_in, gav, gup,
    hs, hr, ks, kr, ds_, dr, ls, lr, as_, ar, ts, tr, ws, wr, es,
):
    me = lax.axis_index("seq")
    fs = lax.axis_index("fsdp")
    x_lo, z, c = me // 8, (me // 2) % 4, me % 2
    y, x_hi = fs // 2, fs % 2
    group = z * 2 + c
    zp, zm, zo = (z + 1) % 4, (z + 3) % 4, (z + 2) % 4
    pending = []

    def col(zz, cc):
        return {"seq": (x_lo * 4 + zz) * 2 + cc, "fsdp": fs}

    def x_neighbour(step):
        xx = (x_hi * 2 + x_lo + step) % 4
        return {"seq": ((xx % 2) * 4 + z) * 2 + c, "fsdp": y * 2 + xx // 2}

    sibling = col(z, 1 - c)
    partner = {"seq": (me + 8) % 16, "fsdp": fs}

    def send(src, dst, s, r, device):
        copy = remote(src, dst, s, r, device)
        copy.start()
        pending.append(copy)

    def arrived(region, s, r):
        remote(region, region, s, r, sibling).wait_recv()

    loads = []
    for g in range(8):
        for h in range(2):
            copy = pltpu.make_async_copy(
                e_hbm.at[pl.ds(128 * (8 * h + g), 128), :],
                ep.at[pl.ds(256 * g + 128 * h, 128), :],
                es.at[2 * g + h],
            )
            copy.start()
            loads.append(copy)

    barrier = pltpu.get_barrier_semaphore()
    for d in range(1, 16):
        pl.semaphore_signal(
            barrier, inc=1, device_id={"seq": (me + d) % 16, "fsdp": fs}, device_id_type=MESH
        )
    outer = x_neighbour(jnp.where(x_lo == 0, -1, 1) + 4)
    pl.semaphore_signal(barrier, inc=1, device_id=outer, device_id_type=MESH)

    low_half = lax.broadcasted_iota(jnp.int32, (128, 128), 1) < 64

    own_w = pl.multiple_of(x_lo * 384, 128)

    def permute(i, _):
        rows = pl.ds(pl.multiple_of(i * 128, 128), 128)
        t0 = w_in[rows, 0:128].astype(F32)
        t1 = w_in[rows, 128:256].astype(F32)
        t2 = w_in[rows, 256:384].astype(F32)
        keys = pltpu.roll(jnp.where(low_half, t2, t0), 64, 1)
        wall[rows, pl.ds(own_w, 128)] = jnp.where(low_half, t0, t1).astype(BF16)
        wall[rows, pl.ds(own_w + 128, 128)] = keys.astype(BF16)
        wall[rows, pl.ds(own_w + 256, 128)] = jnp.where(low_half, t1, t2).astype(BF16)
        return 0

    lax.fori_loop(0, WIDTH // 128, permute, 0)

    def hid_rows(k, s, zz, cc, start=0, size=64):
        return hid.at[k, s, pl.ds(pl.multiple_of(64 * (2 * zz + cc) + start, 32), size), :]

    own_rows = pl.ds(pl.multiple_of(64 * group, 64), 64)

    def norm(k, s, x):
        power = jnp.mean(x * x, axis=-1, keepdims=True)
        h = (x * lax.rsqrt(power + EPS) * gains[...].astype(F32)).astype(BF16)
        hid[k, s, own_rows, :] = h

    def gather_start(k, s):
        p = 2 * k + s
        own = hid_rows(k, s, z, c)
        send(own, own, hs.at[p, 1], hr.at[p, 1], col(zp, c))
        send(own, own, hs.at[p, 2], hr.at[p, 2], col(zm, c))
        send(own, own, hs.at[p, 0], hr.at[p, 0], sibling)

    def gather_near(k, s):
        p = 2 * k + s
        below, above = hid_rows(k, s, zm, c), hid_rows(k, s, zp, c)
        arrived(below, hs.at[p, 1], hr.at[p, 1])
        half = hid_rows(k, s, zm, c, 0, 32)
        send(half, half, hs.at[p, 4], hr.at[p, 4], col(zp, c))
        send(below, below, hs.at[p, 3], hr.at[p, 3], sibling)
        arrived(above, hs.at[p, 2], hr.at[p, 2])
        half = hid_rows(k, s, zp, c, 32, 32)
        send(half, half, hs.at[p, 6], hr.at[p, 6], col(zm, c))
        send(above, above, hs.at[p, 5], hr.at[p, 5], sibling)

    def gather_far(k, s):
        p = 2 * k + s
        for n, start in ((4, 0), (6, 32)):
            half = hid_rows(k, s, zo, c, start, 32)
            arrived(half, hs.at[p, n], hr.at[p, n])
            m = 7 if n == 4 else 8
            send(half, half, hs.at[p, m], hr.at[p, m], sibling)

    def project(k, s, j):
        p = 2 * k + s
        zz = (z, zm, zp, zo)[j]
        if j == 0:
            arrived(hid_rows(k, s, z, 1 - c), hs.at[p, 0], hr.at[p, 0])
        elif j == 1:
            arrived(hid_rows(k, s, zm, 1 - c), hs.at[p, 3], hr.at[p, 3])
        elif j == 2:
            arrived(hid_rows(k, s, zp, 1 - c), hs.at[p, 5], hr.at[p, 5])
        else:
            arrived(hid_rows(k, s, zo, 1 - c, 0, 32), hs.at[p, 7], hr.at[p, 7])
            arrived(hid_rows(k, s, zo, 1 - c, 32, 32), hs.at[p, 8], hr.at[p, 8])
        base = pl.multiple_of(128 * zz, 128)
        rows = pl.ds(base, 128)
        there = pl.ds(pl.multiple_of(x_lo * 512 + 128 * zz, 128), 128)
        h = hid[k, s, rows, :]
        low = mm(h, vred[...])
        lowvt[k, s, x_lo, :, rows] = low.T.astype(BF16)
        add = mm(low.astype(BF16), lift2[...])
        mixed = mm(h, wall[...])
        q[s, rows, 0:128] = mixed[:, 0:128].astype(BF16)
        q[s, rows, 128:256] = mixed[:, 384:512].astype(BF16)
        kv[k, s, there, 0:128] = mixed[:, 128:256].astype(BF16)
        kv[k, s, there, 128:256] = (mixed[:, 256:384] + add[:, 0:128]).astype(BF16)
        kv[k, s, there, 256:384] = mixed[:, 512:640].astype(BF16)
        kv[k, s, there, 384:512] = (mixed[:, 640:768] + add[:, 128:256]).astype(BF16)
        region = kv.at[k, s, there, :]
        send(region, region, ks.at[p, j], kr.at[p, j], partner)
        if j == 3:
            region = lowvt.at[k, s, x_lo]
            send(region, region, ks.at[p, 4], kr.at[p, 4], partner)

    def attention(k, s):
        p = 2 * k + s
        for j in range(4):
            zz = (z, zm, zp, zo)[j]
            there = pl.ds(pl.multiple_of((1 - x_lo) * 512 + 128 * zz, 128), 128)
            arrived(kv.at[k, s, there, :], ks.at[p, j], kr.at[p, j])
        arrived(lowvt.at[k, s, 1 - x_lo], ks.at[p, 4], kr.at[p, 4])
        for n in range(2):
            vt[n] = kv[k, s, :, 256 * n + 128:256 * n + 256].astype(F32).T.astype(BF16)
        dv[...] = jnp.zeros_like(dv)
        head_of = lax.broadcasted_iota(jnp.int32, (256, 128), 1) < 64

        def tile(i, _):
            n, t = i // 2, i % 2
            rows = pl.ds(pl.multiple_of(t * 256, 256), 256)
            lanes = pl.ds(pl.multiple_of(n * 128, 128), 128)
            q2 = q[s, rows, lanes].astype(F32) * 0.125
            do2 = dout[p, rows, lanes].astype(F32)
            k2 = kv[k, s, :, pl.ds(pl.multiple_of(n * 256, 128), 128)]
            outs = []
            total = None
            for h in range(2):
                mask = head_of if h == 0 else jnp.logical_not(head_of)
                st = mm_nt(k2, jnp.where(mask, q2, 0.0).astype(BF16))
                e = jnp.exp(st - jnp.max(st, axis=0, keepdims=True))
                probs = (e * (1.0 / jnp.sum(e, axis=0, keepdims=True))).astype(BF16)
                outs.append(mm(vt[n, 64 * h:64 * h + 64, :], probs))
                term = mm(probs, jnp.where(mask, do2, 0.0).astype(BF16))
                total = term if total is None else total + term
            dv[:, lanes] += total
            att_src[k, s, rows, lanes] = jnp.concatenate(outs, axis=0).T.astype(BF16)
            return 0

        lax.fori_loop(0, 4, tile, 0)
        mine = pl.ds(pl.multiple_of(256 * group, 256), 256)
        for d in range(1, 8):
            g = (group + d) % 8
            send(
                att_src.at[k, s, pl.ds(pl.multiple_of(64 * g, 64), 64), :],
                att.at[k, s, :, mine],
                as_.at[p, d],
                ar.at[p, d],
                {"seq": x_lo * 8 + g, "fsdp": fs},
            )
        att[k, s, :, mine] = att_src[k, s, own_rows, :]

    def values_gradient(k, s):
        dvb = dv[...].astype(BF16)
        r2_out[0:32, :] += mm(lowvt[k, s, 0], dvb[0:512]) + mm(lowvt[k, s, 1], dvb[512:1024])
        dlv[s] = mm_nt(lift2[...], dvb)

    def send_low_values(k):
        lower = lax.broadcasted_iota(jnp.int32, (32, 128), 1) < 64
        for j in range(8):
            b0, b1 = dlv[0, :, 128 * j:128 * j + 128], dlv[1, :, 128 * j:128 * j + 128]
            dl_src[k, 2 * j] = jnp.where(lower, b0, pltpu.roll(b1, 64, 1))
            dl_src[k, 2 * j + 1] = jnp.where(lower, pltpu.roll(b0, 64, 1), b1)
        for d in range(1, 16):
            to = (me + d) % 16
            send(
                dl_src.at[k, to], dl_in.at[k, d], ts.at[k, d], tr.at[k, d], {"seq": to, "fsdp": fs}
            )

    def reducer_gradient(k):
        total = jnp.zeros((32, 256), F32)
        for g in range(8):
            both = jnp.concatenate(
                [att_src[k, 0, 64 * g:64 * g + 64, :], att_src[k, 1, 64 * g:64 * g + 64, :]], axis=0
            )
            total = total + mm(dlo[g, 32 * k:32 * k + 32, :], both)
        r2_out[32:64, :] += total

    def down_gradient(k):
        total = dl_src[k, me]
        for d in range(1, 16):
            arrived(dl_in.at[k, d], ts.at[k, d], tr.at[k, d])
            total = total + dl_in[k, d]
        both = jnp.concatenate([hid[k, 0, own_rows, :], hid[k, 1, own_rows, :]], axis=0)
        gav[...] += mm(total.astype(BF16), both)

    def outlet(k, s):
        p = 2 * k + s
        for d in range(1, 8):
            g = (group + 8 - d) % 8
            region = att.at[k, s, :, pl.ds(pl.multiple_of(256 * g, 256), 256)]
            arrived(region, as_.at[p, d], ar.at[p, d])
        keep, push, spread = plan(k)
        a = att[k, s]
        low = mm(a, redp[...])
        lowb = low.astype(BF16)
        rows = slice(128 * k + 64 * s, 128 * k + 64 * s + 64)
        gup[...] += mm(low.T.astype(BF16), dvel[rows, :])
        for start in range(0, WIDTH, 512):
            stop = min(start + 512, WIDTH)
            v = mm(a, ep[:, start:stop]) + mm(lowb, olift[:, start:stop])
            old = x0[s, :, start:stop] if k == 0 else x_out[s, :, start:stop]
            x_out[s, :, start:stop] = keep * old + push * v + spread * draws[k, s, :, start:stop]

    norm(0, 0, x0[0])
    norm(0, 1, x0[1])
    pl.semaphore_wait(barrier, 16)
    gather_start(0, 0)
    half = WIDTH // 2
    for n, step in ((0, 1), (1, 3)):
        region = wall.at[pl.ds(n * half, half), pl.ds(own_w, 384)]
        send(region, region, ws.at[n], wr.at[n], x_neighbour(step))
    gather_start(0, 1)

    lift2[:, 0:128] = vlift[:, pl.ds(pl.multiple_of(128 * group, 128), 128)]
    lift2[:, 128:256] = vlift[:, pl.ds(pl.multiple_of(1024 + 128 * group, 128), 128)]
    for g in range(8):
        for h in range(2):
            redp[256 * g + 128 * h:256 * g + 128 * h + 128, :] = ored[
                128 * (8 * h + g):128 * (8 * h + g) + 128, :
            ]
    r2_out[...] = jnp.zeros_like(r2_out)
    gav[...] = jnp.zeros_like(gav)
    gup[...] = jnp.zeros_like(gup)

    for k in range(2):
        keep, push, spread = plan(k)
        coef = -push / (2.0 * SAMPLES * spread)
        for s in range(2):
            start = 128 * k + 64 * s
            dvel[start:start + 64, :] = ((coef * rewards[s]) * draws[k, s]).astype(BF16)
    low = mm_nt(dvel[...], olift[...])
    lowb = low.astype(BF16)
    low_t = low.T.astype(BF16)
    for k in range(2):
        dlo_src[32 * k:32 * k + 32, :] = low_t[:, 128 * k:128 * k + 128]
    for d in range(1, 8):
        g = (group + d) % 8
        send(dlo_src, dlo.at[group], ls.at[d], lr.at[d], {"seq": x_lo * 8 + g, "fsdp": fs})
    dlo[group] = dlo_src[...]

    gather_near(0, 0)
    for copy in loads:
        copy.wait()

    def outlet_back(g, _):
        rows = pl.ds(pl.multiple_of(256 * g, 256), 256)
        d = mm_nt(dvel[...], ep[rows, :]) + mm_nt(lowb, redp[rows, :])
        dsend[g] = d.astype(BF16).reshape(4, 64, 256)
        return 0

    lax.fori_loop(0, 8, outlet_back, 0)
    gather_near(0, 1)
    gather_far(0, 0)
    for d in range(1, 8):
        g = (group + d) % 8
        send(
            dsend.at[g],
            dout.at[:, own_rows, :],
            ds_.at[d],
            dr.at[d],
            {"seq": x_lo * 8 + g, "fsdp": fs},
        )
    dout[:, own_rows, :] = dsend[group]
    gather_far(0, 1)
    for n in range(2):
        region = wall.at[pl.ds(n * half, half), pl.ds(pl.multiple_of((1 - x_lo) * 384, 128), 384)]
        arrived(region, ws.at[n], wr.at[n])

    for s in range(2):
        for j in range(4):
            project(0, s, j)
    for d in range(1, 8):
        g = (group + 8 - d) % 8
        rows = pl.ds(pl.multiple_of(64 * g, 64), 64)
        arrived(dout.at[:, rows, :], ds_.at[d], dr.at[d])
        arrived(dlo.at[g], ls.at[d], lr.at[d])

    attention(0, 0)
    values_gradient(0, 0)
    outlet(0, 0)
    norm(1, 0, x_out[0])
    gather_start(1, 0)
    attention(0, 1)
    gather_near(1, 0)
    values_gradient(0, 1)
    outlet(0, 1)
    norm(1, 1, x_out[1])
    gather_start(1, 1)
    gather_far(1, 0)
    for j in range(4):
        project(1, 0, j)
    gather_near(1, 1)
    send_low_values(0)
    reducer_gradient(0)
    gather_far(1, 1)
    for j in range(4):
        project(1, 1, j)
    attention(1, 0)
    values_gradient(1, 0)
    down_gradient(0)
    outlet(1, 0)
    attention(1, 1)
    values_gradient(1, 1)
    send_low_values(1)
    reducer_gradient(1)
    outlet(1, 1)
    down_gradient(1)
    r1_out[0:32, :] = gav[...]
    r1_out[32:64, :] = gup[...]
    for copy in pending:
        copy.wait_send()


def sum_kernel(a_ref, r_ref, out, a_in, r_in, b_src, b_in, s1, r1, s2, r2, s3, r3):
    me = lax.axis_index("seq")
    fs = lax.axis_index("fsdp")
    x_lo = me // 8
    pending = []
    barrier = pltpu.get_barrier_semaphore()
    for d in range(1, 16):
        pl.semaphore_signal(
            barrier, inc=1, device_id={"seq": (me + d) % 16, "fsdp": fs}, device_id_type=MESH
        )
    for d in range(1, 8):
        pl.semaphore_signal(
            barrier, inc=1, device_id={"seq": me, "fsdp": (fs + d) % 8}, device_id_type=MESH
        )
    pl.semaphore_wait(barrier, 22)

    def send(src, dst, s, r, device):
        copy = remote(src, dst, s, r, device)
        copy.start()
        pending.append(copy)
        return copy

    first = []
    for d in range(1, 16):
        to = (me + d) % 16
        first.append(
            send(a_ref.at[to], a_in.at[d], s1.at[d], r1.at[d], {"seq": to, "fsdp": fs})
        )
    other = send(
        r_ref.at[:, pl.ds(pl.multiple_of((1 - x_lo) * 128, 128), 128)],
        r_in, s2, r2, {"seq": (me + 8) % 16, "fsdp": fs},
    )
    other.wait_recv()
    b_src[:, 256:384] = r_ref[:, pl.ds(pl.multiple_of(x_lo * 128, 128), 128)] + r_in[...]
    total = a_ref[me]
    for d in range(1, 16):
        first[d - 1].wait_recv()
        total = total + a_in[d]
    b_src[:, 0:256] = total
    second = []
    for d in range(1, 8):
        second.append(
            send(b_src, b_in.at[d], s3.at[d], r3.at[d], {"seq": me, "fsdp": (fs + d) % 8})
        )
    total = b_src[...]
    for d in range(1, 8):
        second[d - 1].wait_recv()
        total = total + b_in[d]
    out[...] = total
    for copy in pending:
        copy.wait_send()


def per_device(
    perturbed_codes,
    random_draws,
    relative_rewards,
    rescaling_gains,
    triple_projector,
    emission_projector,
    payload_bypass_reducer,
    payload_bypass_lift,
    outlet_bypass_reducer,
    outlet_bypass_lift,
):
    vmem = pl.BlockSpec(memory_space=pltpu.VMEM)
    dma = pltpu.SemaphoreType.DMA
    final, r1, r2 = pl.pallas_call(
        block_kernel,
        out_shape=(
            jax.ShapeDtypeStruct((2, 64, WIDTH), F32),
            jax.ShapeDtypeStruct((64, WIDTH), F32),
            jax.ShapeDtypeStruct((64, 256), F32),
        ),
        in_specs=[
            vmem, vmem, pl.BlockSpec(memory_space=pltpu.SMEM), vmem, vmem,
            pl.BlockSpec(memory_space=pl.ANY), vmem, vmem, vmem, vmem,
        ],
        out_specs=(vmem, vmem, vmem),
        scratch_shapes=[
            pltpu.VMEM((WIDTH, 768), BF16),
            pltpu.VMEM((INNER, WIDTH), BF16),
            pltpu.VMEM((2, 2, 512, WIDTH), BF16),
            pltpu.VMEM((2, 512, 256), BF16),
            pltpu.VMEM((2, 2, 1024, 512), BF16),
            pltpu.VMEM((2, 2, 2, RANK, 512), BF16),
            pltpu.VMEM((4, 512, 256), BF16),
            pltpu.VMEM((8, 4, 64, 256), BF16),
            pltpu.VMEM((8, 64, 128), BF16),
            pltpu.VMEM((64, 128), BF16),
            pltpu.VMEM((INNER, RANK), BF16),
            pltpu.VMEM((RANK, 256), BF16),
            pltpu.VMEM((2, 2, 64, INNER), BF16),
            pltpu.VMEM((2, 2, 512, 256), BF16),
            pltpu.VMEM((256, WIDTH), BF16),
            pltpu.VMEM((2, 128, 1024), BF16),
            pltpu.VMEM((1024, 256), F32),
            pltpu.VMEM((2, RANK, 1024), F32),
            pltpu.VMEM((2, 16, RANK, 128), F32),
            pltpu.VMEM((2, 16, RANK, 128), F32),
            pltpu.VMEM((RANK, WIDTH), F32),
            pltpu.VMEM((RANK, WIDTH), F32),
            dma((4, 9)), dma((4, 9)),
            dma((4, 5)), dma((4, 5)),
            dma((8,)), dma((8,)),
            dma((8,)), dma((8,)),
            dma((4, 8)), dma((4, 8)),
            dma((2, 16)), dma((2, 16)),
            dma((2,)), dma((2,)),
            dma((16,)),
        ],
        compiler_params=pltpu.CompilerParams(
            collective_id=0, has_side_effects=True, vmem_limit_bytes=58 * 1024 * 1024
        ),
        name="rollout",
    )(
        perturbed_codes,
        random_draws,
        relative_rewards,
        rescaling_gains.reshape(1, WIDTH),
        triple_projector,
        emission_projector,
        payload_bypass_reducer,
        payload_bypass_lift,
        outlet_bypass_reducer,
        outlet_bypass_lift,
    )
    pieces = jnp.pad(
        r1.reshape(64, 16, WIDTH // 16).transpose(1, 0, 2), ((0, 0), (0, 0), (0, 256 - WIDTH // 16))
    )
    sums = pl.pallas_call(
        sum_kernel,
        out_shape=jax.ShapeDtypeStruct((64, 384), F32),
        in_specs=[vmem, vmem],
        out_specs=vmem,
        scratch_shapes=[
            pltpu.VMEM((16, 64, 256), F32),
            pltpu.VMEM((64, 128), F32),
            pltpu.VMEM((64, 384), F32),
            pltpu.VMEM((8, 64, 384), F32),
            dma((16,)), dma((16,)),
            dma, dma,
            dma((8,)), dma((8,)),
        ],
        compiler_params=pltpu.CompilerParams(
            collective_id=1, has_side_effects=True, vmem_limit_bytes=32 * 1024 * 1024
        ),
        name="gradient_sums",
    )(pieces, r2)
    mine = lax.axis_index("fsdp")
    wide = lax.dynamic_slice(sums, (0, mine * 19), (64, 19))
    narrow = lax.dynamic_slice(sums, (0, 256 + mine * 16), (64, 16))
    return (final, wide[0:32].T, narrow[0:32], narrow[32:64].T, wide[32:64])


def solution(mesh):
    placed = (
        P("fsdp", "seq", None),
        P(None, "fsdp", "seq", None),
        P("fsdp"),
        P(),
        P(None, "seq"),
        P(),
        P(),
        P(),
        P(),
        P(),
    )
    return jax.shard_map(
        per_device,
        mesh=mesh,
        in_specs=placed,
        out_specs=(
            P("fsdp", "seq", None),
            P(("seq", "fsdp"), None),
            P(None, ("seq", "fsdp")),
            P(("seq", "fsdp"), None),
            P(None, ("seq", "fsdp")),
        ),
        check_vma=False,
    )
```

time: 2050 us -> 187 us (0.09); the launches traced: 2030 us -> 186 us
  waiting for transfers between devices: 1570 us -> 0 us
  local copies, waits for them, and re-layouts: 236 us -> 12.4 us
  Pallas kernels: 0 us -> 173 us
  matrix products: 122 us -> 0 us
  other arithmetic: 51 us -> 0 us
  starting transfers between devices: 34 us -> 0 us
    reduce_scatter x2 -> x0, waiting for transfers between devices: 1260 us -> none  [the longest x1 635 us: per_device(): lax.psum_scatter(grad_bv, ('seq', 'fsdp'), scatter_dimension=1, tiled=True)]
    pallas_call x0 -> x2, Pallas kernels: none -> 173 us  [the longest x1 142 us: per_device(): pl.pallas_call(block_kernel, out_shape=(jax.ShapeDtypeStruct((2, 64, WIDT...]
    all_gather x1 -> x0, waiting for transfers between devices: 145 us -> none  [per_device(): full_weight = lax.all_gather(triple_projector, 'seq', axis=1, tiled=True)]
    unnamed x5 -> x0, waiting for transfers between devices: 138 us -> none
    scatter-add x2 -> x0, local copies, waits for them, and re-layouts: 106 us -> none  [per_device(): mixed = mixed.at[:, :, :, 2, :].add(iterate_increment).astype(jnp.bfloat1...]
    dot_general x27 -> x0, matrix products: 103 us -> none  [the longest x2 31 us: per_device(): jnp.einsum('bsd,dc->bsc', hidden_rows, full_weight, preferred_element_typ...]
    reshape x10 -> x3, local copies, waits for them, and re-layouts: 64.2 us -> 4.38 us  [the longest x2 3.08 us: per_device(): r1.reshape(64, 16, WIDTH // 16).transpose(1, 0, 2)]
    all_to_all x6 -> x0, starting transfers between devices: 33.6 us -> none  [the longest x2 11.5 us: per_device(): lax.all_to_all(mixed, 'seq', split_axis=2, concat_axis=1, tiled=True)]
  transfers between devices with their start and end apart: 10 -> 0, of which waited for: 7 -> 0; matrix products, arithmetic and copies ran while one was open for 6% -> 0% of each run, Pallas kernels for 0% -> 0%
where the time goes in v1:
time: 187 us; the launch traced here: 186 us
  Pallas kernels  173 us (93%)
  local copies, waits for them, and re-layouts  12.4 us (7%)
    pallas_call x1, Pallas kernels, per_device(): pl.pallas_call(block_kernel, out_shape=(jax.ShapeDtypeStruct((2, 64, WIDT...  142 us
    pallas_call x1, Pallas kernels, per_device(): pl.pallas_call(sum_kernel, out_shape=jax.ShapeDtypeStruct((64, 384), F32)...  30.9 us
    unnamed x11, local copies, waits for them, and re-layouts  7.76 us

profile of v1, /device:TPU:1, one launch (start us, length us, event | category | flops | bytes accessed | tf_op | source)
XLA Modules:
  0.0 186.0 jit_solution(7740218309830892712)
XLA Ops:
  0.6 1.3 reshape.16.gains
  1.9 2.0 %copy.21.vred = bf16[2432,32]{1,0:T(8,128)(2,1)} copy(bf16[2432,32]{0,1:T(8,128)(2,1)} %param.16) | data formatting | bytes 311296 | tf_op args[6]
  3.9 1.9 %copy.22.ored = bf16[2048,32]{1,0:T(8,128)(2,1)} copy(bf16[2048,32]{0,1:T(8,128)(2,1)} %param.18) | data formatting | bytes 262144 | tf_op args[8]
  5.8 142.1 %rollout.1 = (f32[2,64,2432]{2,1,0:T(8,128)}, f32[64,2432]{1,0:T(8,128)}, f32[64,256]{1,0:T(8,128)}) custom-call(f32[2,64,2432]{2,1,0:T(8,128)} %x0.1, f32[2,2,64,2432]{3,2,1,0:T(8,128)} %draws.1, f32[2]{0:T(128)} %rewards.1, bf16[1,2432]{1,0:T(2,128)(2,1)} %reshape.16.gains, bf16[2432,384]{1,0:T(8,128)(2,1)} %w_in.1, bf16[2048,2432]{1,0:T(8,128)(2,1)} %e_hbm.1, ...), custom_call_target="tpu_custom_call" | custom-call | tf_op jit(solution)/shard_map/rollout/pallas_call | solution.py:467
  147.9 2.5 %reshape.17 = f32[64,16,152]{2,1,0:T(8,128)S(1)} reshape(f32[64,2432]{1,0:T(8,128)} %get-tuple-element.9) | data formatting | bytes 1245184 | tf_op jit(solution)/shard_map/reshape | solution.py:528
  150.4 0.0 copy-start
  150.4 0.6 copy.29
  151.0 0.0 copy-start.1
  151.0 0.1 pad.4.a_ref
  151.1 0.1 copy-done
  151.2 30.9 %gradient_sums.1 = f32[64,384]{1,0:T(8,128)S(1)} custom-call(f32[16,64,256]{2,1,0:T(8,128)S(1)} %pad.4.a_ref, f32[64,256]{1,0:T(8,128)S(1)} %copy-done), custom_call_target="tpu_custom_call" | custom-call | tf_op jit(solution)/shard_map/gradient_sums/pallas_call | solution.py:530
  182.1 0.1 fusion
  182.2 0.7 copy.24
  182.9 0.1 dynamic-slice_bitcast_fusion
  183.0 0.7 copy.25
  183.7 0.7 copy.26
  184.3 0.7 copy.27
  185.0 0.0 copy-done.1
  185.0 1.0 copy.31
Async XLA Ops:
  150.4 0.8 copy-start
  151.0 34.0 %copy-start.1 = (f32[2,64,2432]{2,1,0:T(8,128)S(1)}, f32[2,64,2432]{2,1,0:T(8,128)}, u32[]{:S(2)}) copy-start(f32[2,64,2432]{2,1,0:T(8,128)} %get-tuple-element.30) | copy-start | bytes 3735556
